TPU v7x, 512 devices: a whole 4x4x16 slice. The times are simulated.
512 devices in a mesh: agent: 4 (over x_hi, core), expert: 128 (over y, x_lo, z).
Axes of the slice: x: 4 (x_hi: 2, x_lo: 2; x = x_hi * 2 + x_lo), y: 4, z: 16, core: 2. Of those that a mesh axis runs over, the one named last changes fastest.
Arguments:
- expert_ids: int32 [4, 16384, 8], P('agent', 'expert'), may hold values from 0 to 127, all different within a row; in each aligned block of 128 rows (0 to 127, 128 to 255, ..., all dimensions but the last counted through in order) at most 12 rows name the same one
- gate_probs: float32 [4, 16384, 8], P('agent', 'expert'), may hold values from 0.03 to 0.3
- cotangent: bfloat16 [4, 16384, 1024], P('agent', 'expert'), may hold values from -0.19921875 to 0.19921875
- hidden: bfloat16 [4, 128, 1536, 384], P('agent', 'expert'), may hold values from -6 to 6
- w_down: bfloat16 [4, 128, 384, 1024], P('agent', 'expert'), may hold values from -0.3125 to 0.3125
- psi_prev: bfloat16 [4, 128, 384, 1024], P('agent', 'expert'), may hold values from -0.3125 to 0.3125
Outputs:
- mixed_out: bfloat16 [4, 16384, 1024], P('agent', 'expert')
- prob_grad: float32 [4, 16384, 8], P('agent', 'expert')
- w_next: bfloat16 [4, 128, 384, 1024], P('agent', 'expert')
- psi_next: bfloat16 [4, 128, 384, 1024], P('agent', 'expert')
Inputs may be any that keep to these rules, and one draw needn't show every extreme that they name: `expert_ids`: each token names 8 different experts. Among the tokens of one device (aligned blocks of 128 rows, agents then tokens) no expert is named more than 12 times, and some expert reaches it.
All inputs are finite; a program needn't handle non-finite values.
Results may differ from a plain program's by a relative error of at most 0.008.
Values may be sent and summed in bfloat16 or wider, within the bound.
A program may use at most 64 MiB of HBM per device.

v0:
```python
import jax
import jax.numpy as jnp
from jax import lax
from jax.sharding import PartitionSpec as P

step_rate = 0.25


def swapped(array, axis, stride):
    return lax.ppermute(array, axis, [(i, i ^ 1 << stride) for i in range(lax.axis_size(axis))])


def slot_ranks(choices, col_count):
    marks_hot = (choices[:, None] == jnp.arange(col_count, dtype=jnp.int32)[None, :]).astype(
        jnp.int32
    )
    running = jnp.cumsum(marks_hot, axis=0)
    return jnp.sum(marks_hot * running, axis=1) - 1


def per_device(expert_ids, gate_probs, cotangent, hidden, w_down, psi_prev):
    groups = lax.axis_size("expert")
    hidden_rows = hidden[0, 0]
    weight = w_down[0, 0]
    slot_count = hidden_rows.shape[0]
    capacity = slot_count // groups
    model_width = weight.shape[1]
    choices = expert_ids[0].reshape(-1)
    target = choices * capacity + slot_ranks(choices, groups)
    gate_share = gate_probs[0]
    grads_in = cotangent[0]
    tok_count = gate_share.shape[0]
    top_count = gate_share.shape[1]
    scaled = (gate_share[:, :, None] * grads_in.astype(jnp.float32)[:, None, :]).astype(
        jnp.bfloat16
    )
    outbound = (
        jnp.zeros((slot_count, model_width), jnp.bfloat16)
        .at[target]
        .set(scaled.reshape(-1, model_width))
    )
    outbound = outbound.reshape(groups, capacity, model_width)
    produced = jnp.dot(hidden_rows, weight, preferred_element_type=jnp.float32).astype(jnp.bfloat16)
    produced = produced.reshape(groups, capacity, model_width)
    arrived = lax.all_to_all(outbound, "expert", split_axis=0, concat_axis=0, tiled=True)
    flat_rows = arrived.reshape(slot_count, arrived.shape[-1])
    gradient = lax.dot_general(
        hidden_rows, flat_rows, (((0,), (0,)), ((), ())), preferred_element_type=jnp.float32
    )
    returned = lax.all_to_all(produced, "expert", split_axis=0, concat_axis=0, tiled=True)
    picked = (
        returned.reshape(slot_count, model_width)[target]
        .astype(jnp.float32)
        .reshape(tok_count, top_count, model_width)
    )
    mixed_out = jnp.sum(gate_share[:, :, None] * picked, axis=1).astype(jnp.bfloat16)
    prob_grad = jnp.sum(grads_in.astype(jnp.float32)[:, None, :] * picked, axis=2)
    weight_f = weight.astype(jnp.float32)
    psi_next = (weight_f - step_rate * gradient).astype(jnp.bfloat16)
    base_part = weight_f - psi_prev[0, 0].astype(jnp.float32)
    own_phi = psi_next.astype(jnp.float32) + base_part
    partner_phi = swapped(own_phi, "agent", 1)
    w_next = (0.5 * (own_phi + partner_phi)).astype(jnp.bfloat16)
    return (mixed_out[None], prob_grad[None], w_next[None, None], psi_next[None, None])


def solution(mesh):
    return jax.shard_map(
        per_device,
        mesh=mesh,
        in_specs=(
            P("agent", "expert", None),
            P("agent", "expert", None),
            P("agent", "expert", None),
            P("agent", "expert", None, None),
            P("agent", "expert", None, None),
            P("agent", "expert", None, None),
        ),
        out_specs=(
            P("agent", "expert", None),
            P("agent", "expert", None),
            P("agent", "expert", None, None),
            P("agent", "expert", None, None),
        ),
        check_vma=False,
    )
```

profile of v0, /device:TPU:64, one launch (start us, length us, event | category | flops | bytes accessed | tf_op | source)
XLA Modules:
  0.0 448.8 jit_solution(17296980909143087335)
XLA Ops:
  0.7 0.8 broadcast_multiply_fusion
  1.5 0.8 copy.29
  2.7 0.2 fusion.15
  3.1 0.4 fusion.14
  3.8 7.8 %scatter_custom_fusion = bf16[1536,1024]{1,0:T(8,128)(2,1)} fusion(s32[1024]{0:T(1024)S(1)} %bitcast.53, f32[1024]{0:T(1024)S(1)} %mul.81, f32[128,1024]{1,0:T(8,128)S(1)} %bitcast_convert_fusion, bf16[]{:T(256)} %constant.7.clone.1), kind=kCustom, calls=%fused_computation.9 | custom fusion | flops 2097152 | bytes 3674114 | tf_op jit(solution)/shard_map/scatter | solution.py:40
  11.6 6.1 %reshape.111 = bf16[128,12,1024]{2,1,0:T(8,128)(2,1)} reshape(bf16[1536,1024]{1,0:T(8,128)(2,1)} %scatter_custom_fusion) | data formatting | bytes 6291456 | tf_op jit(solution)/shard_map/reshape | solution.py:42
  17.7 20.2 %all-to-all-start.1 = ((bf16[128,12,1024]{2,1,0:T(8,128)(2,1)}), bf16[128,12,1024]{2,1,0:T(8,128)(2,1)}, u32[]{:S(2)}, u32[]{:S(2)}) async-start(bf16[128,12,1024]{2,1,0:T(8,128)(2,1)} %reshape.111), calls=%async_computation.1 | async-start | bytes 8388608 | tf_op jit(solution)/shard_map/all_to_all | solution.py:45
  37.9 3.5 convolution_convert_fusion
  41.4 6.1 %reshape.108 = bf16[128,12,1024]{2,1,0:T(8,128)(2,1)} reshape(bf16[1536,1024]{1,0:T(8,128)(2,1)} %convolution_convert_fusion) | data formatting | bytes 6291456 | tf_op jit(solution)/shard_map/reshape | solution.py:44
  47.5 181.4 %all-to-all-done.1 = bf16[128,12,1024]{2,1,0:T(8,128)(2,1)} async-done(((bf16[128,12,1024]{2,1,0:T(8,128)(2,1)}), bf16[128,12,1024]{2,1,0:T(8,128)(2,1)}, u32[]{:S(2)}, u32[]{:S(2)}) %all-to-all-start.1) | async-done | bytes 3145760 | tf_op jit(solution)/shard_map/all_to_all | solution.py:45
  228.9 6.7 %all-to-all-start = ((bf16[128,12,1024]{2,1,0:T(8,128)(2,1)}), bf16[128,12,1024]{2,1,0:T(8,128)(2,1)}, u32[]{:S(2)}, u32[]{:S(2)}) async-start(bf16[128,12,1024]{2,1,0:T(8,128)(2,1)} %reshape.108), calls=%async_computation | async-start | bytes 8388608 | tf_op jit(solution)/shard_map/all_to_all | solution.py:50
  235.6 1.2 copy.27
  236.8 1.2 copy.34
  237.9 6.3 %reshape.112 = bf16[1536,1024]{1,0:T(8,128)(2,1)} reshape(bf16[128,12,1024]{2,1,0:T(8,128)(2,1)} %all-to-all-done.1) | data formatting | bytes 6291456 | tf_op jit(solution)/shard_map/reshape | solution.py:46
  244.2 5.3 %fusion.8 = (f32[384,1024]{0,1:T(8,128)}, bf16[384,1024]{0,1:T(8,128)(2,1)}) fusion(bf16[1,1,384,1024]{2,3,1,0:T(8,128)(2,1)S(1)} %copy-done.5, bf16[1,1,384,1024]{2,3,1,0:T(8,128)(2,1)S(1)} %copy-done.4, bf16[1536,1024]{1,0:T(8,128)(2,1)} %reshape.112, bf16[1,1,1536,384]{3,2,1,0:T(8,128)(2,1)S(1)} %copy-done), kind=kOutput, calls=%fused_computation.15 | convolution fusion | flops 1211105280 | bytes 8257536 | tf_op jit(solution)/shard_map/dot_general | solution.py:47
  249.5 4.6 %collective-permute-start = (f32[384,1024]{0,1:T(8,128)}, f32[384,1024]{0,1:T(8,128)}, u32[]{:S(2)}, u32[]{:S(2)}) collective-permute-start(f32[384,1024]{0,1:T(8,128)} %get-tuple-element.18), channel_id=1, source_target_pairs={{0,256},{128,384},{256,0},{384,128},{1,257},{129,385},{257,1},{385... | collective-permute-start | bytes 4718600 | tf_op jit(solution)/shard_map/ppermute | solution.py:10
  254.2 171.5 %all-to-all-done = bf16[128,12,1024]{2,1,0:T(8,128)(2,1)} async-done(((bf16[128,12,1024]{2,1,0:T(8,128)(2,1)}), bf16[128,12,1024]{2,1,0:T(8,128)(2,1)}, u32[]{:S(2)}, u32[]{:S(2)}) %all-to-all-start) | async-done | bytes 3145760 | tf_op jit(solution)/shard_map/all_to_all | solution.py:50
  425.7 6.2 %reshape.109 = bf16[1536,1024]{1,0:T(8,128)(2,1)} reshape(bf16[128,12,1024]{2,1,0:T(8,128)(2,1)} %all-to-all-done) | data formatting | bytes 6291456 | tf_op jit(solution)/shard_map/reshape | solution.py:52
  431.9 7.3 %gather_fusion = bf16[1024,1024]{1,0:T(8,128)(2,1)S(1)} fusion(bf16[1536,1024]{1,0:T(8,128)(2,1)} %reshape.109, s32[1024]{0:T(1024)S(1)} %broadcast_clamp_fusion), kind=kCustom, calls=%fused_computation | custom fusion | bytes 4198400 | tf_op jit(solution)/shard_map/gather | solution.py:52
  439.1 3.4 fusion.1
  442.6 0.7 copy.35
  443.2 2.3 copy.37
  445.5 2.1 fusion.12
  447.6 1.2 copy.36
  (34 shorter events, 1.1 us)
Async XLA Ops:
  0.6 37.3 %copy-start = (bf16[1,1,1536,384]{3,2,1,0:T(8,128)(2,1)S(1)}, bf16[1,1,1536,384]{3,2,1,0:T(8,128)(2,1)}, u32[]{:S(2)}) copy-start(bf16[1,1,1536,384]{3,2,1,0:T(8,128)(2,1)} %param.9) | copy-start | bytes 3538948
  0.6 2.9 copy-start.6
  2.5 1.1 copy-start.7
  3.6 14.1 %copy-start.1 = (f32[128,1024]{1,0:T(8,128)}, f32[128,1024]{1,0:T(8,128)S(1)}, u32[]{:S(2)}) copy-start(f32[128,1024]{1,0:T(8,128)S(1)} %bitcast_convert_fusion) | copy-start | bytes 1572868
  17.7 20.3 %copy-start.2 = (bf16[1,1,384,1024]{3,2,1,0:T(8,128)(2,1)S(1)}, bf16[1,1,384,1024]{3,2,1,0:T(8,128)(2,1)}, u32[]{:S(2)}) copy-start(bf16[1,1,384,1024]{3,2,1,0:T(8,128)(2,1)} %param.10) | copy-start | bytes 2359300
  17.7 211.2 %all-to-all-start.1 = ((bf16[128,12,1024]{2,1,0:T(8,128)(2,1)}), bf16[128,12,1024]{2,1,0:T(8,128)(2,1)}, u32[]{:S(2)}, u32[]{:S(2)}) async-start(bf16[128,12,1024]{2,1,0:T(8,128)(2,1)} %reshape.111), calls=%async_computation.1 | async-start | bytes 8388608 | tf_op jit(solution)/shard_map/all_to_all | solution.py:45
  228.9 196.8 %all-to-all-start = ((bf16[128,12,1024]{2,1,0:T(8,128)(2,1)}), bf16[128,12,1024]{2,1,0:T(8,128)(2,1)}, u32[]{:S(2)}, u32[]{:S(2)}) async-start(bf16[128,12,1024]{2,1,0:T(8,128)(2,1)} %reshape.108), calls=%async_computation | async-start | bytes 8388608 | tf_op jit(solution)/shard_map/all_to_all | solution.py:50
  235.6 1.2 copy-start.3
  237.9 6.3 %copy-start.4 = (bf16[1,1,384,1024]{2,3,1,0:T(8,128)(2,1)S(1)}, bf16[1,1,384,1024]{2,3,1,0:T(8,128)(2,1)}, u32[]{:S(2)}) copy-start(bf16[1,1,384,1024]{2,3,1,0:T(8,128)(2,1)} %copy.27) | copy-start | bytes 2359300
  237.9 6.3 %copy-start.5 = (bf16[1,1,384,1024]{2,3,1,0:T(8,128)(2,1)S(1)}, bf16[1,1,384,1024]{2,3,1,0:T(8,128)(2,1)}, u32[]{:S(2)}) copy-start(bf16[1,1,384,1024]{2,3,1,0:T(8,128)(2,1)} %copy.34) | copy-start | bytes 2359300
  249.5 196.1 %collective-permute-start = (f32[384,1024]{0,1:T(8,128)}, f32[384,1024]{0,1:T(8,128)}, u32[]{:S(2)}, u32[]{:S(2)}) collective-permute-start(f32[384,1024]{0,1:T(8,128)} %get-tuple-element.18), channel_id=1, source_target_pairs={{0,256},{128,384},{256,0},{384,128},{1,257},{129,385},{257,1},{385... | collective-permute-start | bytes 4718600 | tf_op jit(solution)/shard_map/ppermute | solution.py:10
where the time goes:
time: 450 us; the launch traced here: 449 us
  waiting for transfers between devices  353 us (78%)
  local copies, waits for them, and re-layouts  40 us (9%)
  starting transfers between devices  31.6 us (7%)
  other arithmetic  14.8 us (3%)
  matrix products  8.74 us (2%)
    all_to_all x1, waiting for transfers between devices, per_device(): lax.all_to_all(outbound, 'expert', split_axis=0, concat_axis=0, tiled=True)  181 us
    all_to_all x1, waiting for transfers between devices, per_device(): lax.all_to_all(produced, 'expert', split_axis=0, concat_axis=0, tiled=True)  171 us
    all_to_all x1, starting transfers between devices, per_device(): lax.all_to_all(outbound, 'expert', split_axis=0, concat_axis=0, tiled=True)  20.2 us
  transfers between devices with their start and end apart: 3, of which 2 were waited for; matrix products, arithmetic and copies ran while one was open for 10% of the time, Pallas kernels for 0%

commit v1 on v0

v1 whole, which is shorter than its diff:
```python
import jax
import jax.numpy as jnp
from jax import lax
from jax.experimental import pallas as pl
from jax.experimental.pallas import tpu as pltpu
from jax.sharding import PartitionSpec as P

Z, Y, X = 16, 4, 2
Q = Y * X
BATCH = 4
BATCHES = Z // BATCH
HALF = Z // 2
STEP_RATE = 0.25
BF, F32 = jnp.bfloat16, jnp.float32


def kernel(
    ids_ref, gates_ref, cot_ref, hidden_ref, weight_ref, prev_ref,
    mixed_ref, prob_ref, next_ref, psi_ref,
    cbuf, meta, prod, rbuf, obuf, rx, mt, key_buf, part, pg, rs_out, rs_in, pg_out, pg_in, phi, phi_out, phi_in,
    ag_send, ag_recv, meta_send, meta_recv, r_send, r_recv, o_send, o_recv,
    rs_send, rs_recv, pg_send, pg_recv, phi_send, phi_recv,
):
    tok, width = cot_ref.shape
    top = ids_ref.shape[0]
    cap = hidden_ref.shape[0] // (Q * Z)
    rows = BATCH * cap
    half = tok // 2
    agent = lax.axis_index("agent")
    me = lax.axis_index("expert")
    z = lax.rem(me, Z)
    column = lax.div(me, Z)
    x = lax.rem(column, X)
    y = lax.div(column, X)

    def on_ring(offset):
        return {"expert": column * Z + lax.rem(z + offset + Z, Z)}

    def peer_column(p):
        dy, dx = p // X, p % X
        return lax.rem(y + dy, Y) * X + lax.rem(x + dx, X)

    def in_plane(p):
        return {"expert": peer_column(p) * Z + z}

    partner = {"agent": lax.rem(agent + 2, 4)}

    def block(offset):
        return lax.rem(z + offset + 2 * Z, Z)

    barrier = pltpu.get_barrier_semaphore()
    peers = [on_ring(1), on_ring(-1), partner] + [in_plane(p) for p in range(1, Q)]
    for peer in peers:
        pl.semaphore_signal(barrier, inc=1, device_id=peer, device_id_type=pl.DeviceIdType.MESH)
    pl.semaphore_wait(barrier, len(peers))

    def remote(src, dst, send, recv, peer):
        return pltpu.make_async_remote_copy(
            src_ref=src, dst_ref=dst, send_sem=send, recv_sem=recv, device_id=peer,
            device_id_type=pl.DeviceIdType.MESH,
        )

    def gather_copy(way, step, piece):
        there = block(-(step - 1) if way == 0 else step - 1)
        place = cbuf.at[there, pl.ds(piece * half, half), :]
        src = cot_ref.at[pl.ds(piece * half, half), :] if step == 1 else place
        return remote(src, place, ag_send.at[way, step - 1, piece], ag_recv.at[way, step - 1, piece],
                      on_ring(1 if way == 0 else -1))

    def meta_copy(way, step):
        place = meta.at[block(-(step - 1) if way == 0 else step - 1)]
        return remote(place, place, meta_send.at[way, step - 1], meta_recv.at[way, step - 1],
                      on_ring(1 if way == 0 else -1))

    def gather_pieces(step):
        if step == HALF:
            return [(0, 0), (1, 1)]
        return [(0, 0), (1, 1), (0, 1), (1, 0)]

    def meta_ways(step):
        return [0] if step == HALF else [0, 1]

    def gather_step(step):
        for way in meta_ways(step):
            if step > 1:
                meta_copy(way, step - 1).wait_recv()
            meta_copy(way, step).start()
        for way, piece in gather_pieces(step):
            if step > 1:
                gather_copy(way, step - 1, piece).wait_recv()
            gather_copy(way, step, piece).start()
        if step > 1:
            for way, piece in gather_pieces(step - 1):
                if (way, piece) not in gather_pieces(step):
                    gather_copy(way, step - 1, piece).wait_recv()
            for way in meta_ways(step - 1):
                if way not in meta_ways(step):
                    meta_copy(way, step - 1).wait_recv()

    meta[z, 0:top, :] = ids_ref[...].astype(F32)
    meta[z, top:2 * top, :] = gates_ref[...]
    gather_step(1)
    cbuf[z] = cot_ref[...]

    def rows_copy(p):
        return remote(prod.at[peer_column(p)], rbuf.at[column], r_send.at[p], r_recv.at[p], in_plane(p))

    def produce(p):
        there = peer_column(p)
        start = pl.multiple_of(there * Z * cap, Z * cap)
        out = jnp.dot(hidden_ref[pl.ds(start, Z * cap), :], weight_ref[...], preferred_element_type=F32).astype(BF)
        if p == 0:
            rbuf[column] = out
        else:
            prod[there] = out
            rows_copy(p).start()

    for p in list(range(1, Q)) + [0]:
        produce(p)

    lane = lax.broadcasted_iota(jnp.int32, (tok, tok), 1)
    sub = lax.broadcasted_iota(jnp.int32, (tok, tok), 0)
    earlier = (sub < lane).astype(F32).astype(BF)
    expert_of = (lax.broadcasted_iota(jnp.int32, (Q, tok), 0) * Z + z).astype(F32)
    row_of = lax.broadcasted_iota(jnp.int32, (rows, tok), 0).astype(F32)

    near = 1 - 2 * lax.div(3 - lax.rem(z, BATCH), 2)
    first = lax.div(z, BATCH)

    def batch_at(order):
        shift = [0, near, -near, 2][order]
        return lax.rem(first + shift + BATCHES, BATCHES)

    def slots(order):
        return pl.ds(pl.multiple_of(batch_at(order) * rows, rows), rows)

    def out_copy(order, p):
        return remote(obuf.at[peer_column(p), slots(order), :], rx.at[column, slots(order), :],
                      o_send.at[order, p], o_recv.at[order, p], in_plane(p))

    def select(order):
        batch = batch_at(order)
        named, weights = [], []
        for i in range(BATCH):
            ids = meta[batch * BATCH + i, 0:top, :]
            gates = meta[batch * BATCH + i, top:2 * top, :]
            hit = jnp.zeros((Q, tok), F32)
            share = jnp.zeros((Q, tok), F32)
            for k in range(top):
                same = ids[k:k + 1, :] == expert_of
                hit = hit + jnp.where(same, 1.0, 0.0)
                share = share + jnp.where(same, gates[k:k + 1, :], 0.0)
            named.append(hit)
            weights.append(share)
        rank = jnp.dot(jnp.concatenate(named, axis=0).astype(BF), earlier, preferred_element_type=F32)
        for i in range(BATCH):
            key = jnp.where(named[i] > 0.5, rank[i * Q:(i + 1) * Q, :] + float(i * cap), -1.0)
            key_buf[batch * BATCH + i] = key
            for q in range(Q):
                chosen = jnp.where(row_of == key[q:q + 1, :], weights[i][q:q + 1, :], 0.0)
                mt[batch, pl.ds(q * rows, rows), pl.ds(i * tok, tok)] = chosen.astype(BF)

    def dispatch(order):
        batch = batch_at(order)
        select(order)

        def chunk(n, carry):
            cols = pl.ds(pl.multiple_of(n * 256, 256), 256)
            tokens = cbuf[pl.ds(batch * BATCH, BATCH), :, cols].reshape(BATCH * tok, 256)
            out = jnp.dot(mt[batch], tokens, preferred_element_type=F32).astype(BF)
            obuf[:, slots(order), cols] = out.reshape(Q, rows, 256)
            return carry

        lax.fori_loop(0, width // 256, chunk, 0)
        for p in range(1, Q):
            out_copy(order, p).start()
        rx[column, slots(order), :] = obuf[column, slots(order), :]

    def combine(order):
        batch = batch_at(order)

        def chunk(n, carry):
            cols = pl.ds(pl.multiple_of(n * 256, 256), 256)
            arrived = rbuf[:, slots(order), cols].reshape(Q * rows, 256)
            out = lax.dot_general(mt[batch], arrived, (((0,), (0,)), ((), ())), preferred_element_type=F32)
            part[pl.ds(batch * BATCH, BATCH), :, cols] = out.reshape(BATCH, tok, 256)
            return carry

        lax.fori_loop(0, width // 256, chunk, 0)
        for i in range(BATCH):
            source = batch * BATCH + i
            scores = lax.dot_general(
                rbuf[:, slots(order), :].reshape(Q * rows, width), cbuf[source],
                (((1,), (1,)), ((), ())), preferred_element_type=F32,
            )
            key = key_buf[source]
            ids = meta[source, 0:top, :]
            total = jnp.zeros((top, tok), F32)
            for q in range(Q):
                picked = jnp.where(row_of == key[q:q + 1, :], scores[q * rows:(q + 1) * rows, :], 0.0)
                value = jnp.sum(picked, axis=0, keepdims=True)
                total = total + jnp.where(ids == (z + q * Z).astype(F32), value, 0.0)
            pg[source] = total

    gather_step(2)
    gather_step(3)
    gather_step(4)
    dispatch(0)
    gather_step(5)
    gather_step(6)
    dispatch(1)
    gather_step(7)
    gather_step(8)
    dispatch(2)
    for p in range(1, Q):
        rows_copy(p).wait_recv()
    for order in range(3):
        combine(order)
    for way in meta_ways(HALF):
        meta_copy(way, HALF).wait_recv()
    for way, piece in gather_pieces(HALF):
        gather_copy(way, HALF, piece).wait_recv()
    dispatch(3)
    combine(3)

    def scatter_copy(way, step, piece):
        span = pl.ds(piece * half, half)
        return remote(rs_out.at[way, step - 1, span, :], rs_in.at[way, step - 1, span, :],
                      rs_send.at[way, step - 1, piece], rs_recv.at[way, step - 1, piece],
                      on_ring(1 if way == 0 else -1))

    def pg_copy(way, step):
        return remote(pg_out.at[way, step - 1], pg_in.at[way, step - 1], pg_send.at[way, step - 1],
                      pg_recv.at[way, step - 1], on_ring(1 if way == 0 else -1))

    def scatter_pieces(step):
        return [(0, 0), (1, 1)] if step == 1 else [(0, 0), (1, 1), (0, 1), (1, 0)]

    def pg_ways(step):
        return [0] if step == 1 else [0, 1]

    def scatter_step(step):
        for way, piece in scatter_pieces(step):
            there = block(HALF + 1 - step if way == 0 else step - HALF - 1)
            span = pl.ds(piece * half, half)
            value = part[there, span, :]
            if (way, piece) in scatter_pieces(step - 1) and step > 1:
                scatter_copy(way, step - 1, piece).wait_recv()
                value = value + rs_in[way, step - 2, span, :].astype(F32)
            rs_out[way, step - 1, span, :] = value.astype(BF)
            scatter_copy(way, step, piece).start()
        for way in pg_ways(step):
            there = block(HALF + 1 - step if way == 0 else step - HALF - 1)
            value = pg[there]
            if step > 1 and way in pg_ways(step - 1):
                pg_copy(way, step - 1).wait_recv()
                value = value + pg_in[way, step - 2]
            pg_out[way, step - 1] = value
            pg_copy(way, step).start()

    def phi_copy(i):
        span = pl.ds(i * 128, 128)
        return remote(phi_out.at[span, :], phi_in.at[span, :], phi_send.at[i], phi_recv.at[i], partner)

    phis = hidden_ref.shape[1] // 128
    scatter_step(1)
    scatter_step(2)
    scatter_step(3)
    for order in range(BATCHES):
        for p in range(1, Q):
            out_copy(order, p).wait_recv()
    for i in range(phis):
        span = pl.ds(i * 128, 128)
        gradient = lax.dot_general(
            hidden_ref[:, span], rx[...].reshape(Q * Z * cap, width), (((0,), (0,)), ((), ())),
            preferred_element_type=F32,
        )
        weight = weight_ref[span, :].astype(F32)
        psi = (weight - STEP_RATE * gradient).astype(BF)
        psi_ref[span, :] = psi
        own = psi.astype(F32) + (weight - prev_ref[span, :].astype(F32))
        phi[span, :] = own
        phi_out[span, :] = own.astype(BF)
        phi_copy(i).start()
    for step in range(4, HALF + 1):
        scatter_step(step)
    for i in range(phis):
        span = pl.ds(i * 128, 128)
        phi_copy(i).wait_recv()
        next_ref[span, :] = (0.5 * (phi[span, :] + phi_in[span, :].astype(F32))).astype(BF)
    for way, piece in scatter_pieces(HALF):
        scatter_copy(way, HALF, piece).wait_recv()
    for way in pg_ways(HALF):
        pg_copy(way, HALF).wait_recv()
    mixed_ref[...] = (
        part[z] + rs_in[0, HALF - 1].astype(F32) + rs_in[1, HALF - 1].astype(F32)
    ).astype(BF)
    prob_ref[...] = pg[z] + pg_in[0, HALF - 1] + pg_in[1, HALF - 1]

    for step in range(1, HALF + 1):
        for way, piece in gather_pieces(step):
            gather_copy(way, step, piece).wait_send()
        for way in meta_ways(step):
            meta_copy(way, step).wait_send()
        for way, piece in scatter_pieces(step):
            scatter_copy(way, step, piece).wait_send()
        for way in pg_ways(step):
            pg_copy(way, step).wait_send()
    for p in range(1, Q):
        rows_copy(p).wait_send()
        for order in range(BATCHES):
            out_copy(order, p).wait_send()
    for i in range(phis):
        phi_copy(i).wait_send()


def per_device(expert_ids, gate_probs, cotangent, hidden, w_down, psi_prev):
    tok, top = expert_ids.shape[1:]
    width = cotangent.shape[2]
    slot_count, inner = hidden.shape[2:]
    cap = slot_count // (Q * Z)
    rows = BATCH * cap
    vmem = pl.BlockSpec(memory_space=pltpu.VMEM)
    dma = pltpu.SemaphoreType.DMA
    mixed, prob, w_next, psi_next = pl.pallas_call(
        kernel,
        out_shape=(
            jax.ShapeDtypeStruct((tok, width), BF),
            jax.ShapeDtypeStruct((top, tok), F32),
            jax.ShapeDtypeStruct((inner, width), BF),
            jax.ShapeDtypeStruct((inner, width), BF),
        ),
        in_specs=[vmem] * 6,
        out_specs=(vmem,) * 4,
        scratch_shapes=[
            pltpu.VMEM((Z, tok, width), BF),
            pltpu.VMEM((Z, 2 * top, tok), F32),
            pltpu.VMEM((Q, Z * cap, width), BF),
            pltpu.VMEM((Q, Z * cap, width), BF),
            pltpu.VMEM((Q, Z * cap, width), BF),
            pltpu.VMEM((Q, Z * cap, width), BF),
            pltpu.VMEM((BATCHES, Q * rows, BATCH * tok), BF),
            pltpu.VMEM((Z, Q, tok), F32),
            pltpu.VMEM((Z, tok, width), F32),
            pltpu.VMEM((Z, top, tok), F32),
            pltpu.VMEM((2, HALF, tok, width), BF),
            pltpu.VMEM((2, HALF, tok, width), BF),
            pltpu.VMEM((2, HALF, top, tok), F32),
            pltpu.VMEM((2, HALF, top, tok), F32),
            pltpu.VMEM((inner, width), F32),
            pltpu.VMEM((inner, width), BF),
            pltpu.VMEM((inner, width), BF),
            dma((2, HALF, 2)), dma((2, HALF, 2)),
            dma((2, HALF)), dma((2, HALF)),
            dma((Q,)), dma((Q,)),
            dma((BATCHES, Q)), dma((BATCHES, Q)),
            dma((2, HALF, 2)), dma((2, HALF, 2)),
            dma((2, HALF)), dma((2, HALF)),
            dma((inner // 128,)), dma((inner // 128,)),
        ],
        compiler_params=pltpu.CompilerParams(
            collective_id=0, has_side_effects=True, vmem_limit_bytes=60 * 1024 * 1024,
        ),
    )(expert_ids[0].T, gate_probs[0].T, cotangent[0], hidden[0, 0], w_down[0, 0], psi_prev[0, 0])
    return mixed[None], prob.T[None], w_next[None, None], psi_next[None, None]


def solution(mesh):
    return jax.shard_map(
        per_device,
        mesh=mesh,
        in_specs=(
            P("agent", "expert", None),
            P("agent", "expert", None),
            P("agent", "expert", None),
            P("agent", "expert", None, None),
            P("agent", "expert", None, None),
            P("agent", "expert", None, None),
        ),
        out_specs=(
            P("agent", "expert", None),
            P("agent", "expert", None),
            P("agent", "expert", None, None),
            P("agent", "expert", None, None),
        ),
        check_vma=False,
    )
```

time: 450 us -> 129 us (0.29)
  the two profiles are of different devices: /device:TPU:64 before, /device:TPU:8 now
where the time goes in v1:
time: 129 us
  Pallas kernels  122 us (95%)
  local copies, waits for them, and re-layouts  5.96 us (5%)
    pallas_call x1, Pallas kernels, per_device(): pl.pallas_call(kernel, out_shape=(jax.ShapeDtypeStruct((tok, width), BF),...  122 us
    unnamed x6, local copies, waits for them, and re-layouts  5.96 us

profile of v1, /device:TPU:8, one launch (start us, length us, event | category | flops | bytes accessed | tf_op | source)
XLA Modules:
  0.0 128.7 jit_solution(7736845440789750594)
XLA Ops:
  0.6 122.1 %shard_map.93 = (bf16[128,1024]{1,0:T(8,128)(2,1)}, f32[8,128]{1,0:T(8,128)}, bf16[384,1024]{1,0:T(8,128)(2,1)}, bf16[384,1024]{1,0:T(8,128)(2,1)}) custom-call(s32[8,128]{1,0:T(8,128)} %bitcast.23, f32[8,128]{1,0:T(8,128)} %bitcast.24, bf16[128,1024]{1,0:T(8,128)(2,1)} %bitcast.21, bf16[1536,384]{1,0:T(8,128)(2,1)} %bitcast.16, bf16[384,1024]{1,0:T(8,128)(2,1)} %bitcast.19, ...), custom_call_target="tpu_custom_call" | custom-call | tf_op jit(solution)/shard_map/pallas_call | solution.py:325
  122.8 0.0 copy-start
  122.8 1.7 %copy.14 = bf16[1,128,1024]{2,1,0:T(8,128)(2,1)} copy(bf16[1,128,1024]{2,1,0:T(8,128)(2,1)} %bitcast.22) | data formatting | bytes 524288
  124.5 1.3 copy.15
  125.8 2.1 %copy.16 = bf16[1,1,384,1024]{3,2,1,0:T(8,128)(2,1)} copy(bf16[1,1,384,1024]{3,2,1,0:T(8,128)(2,1)} %bitcast.18) | data formatting | bytes 1572864
  127.9 0.0 copy-done
  127.9 0.9 copy.17
Async XLA Ops:
  122.8 5.1 %copy-start = (bf16[384,1024]{1,0:T(8,128)(2,1)S(1)}, bf16[384,1024]{1,0:T(8,128)(2,1)}, u32[]{:S(2)}) copy-start(bf16[384,1024]{1,0:T(8,128)(2,1)} %get-tuple-element.11) | copy-start | bytes 2359300

commit v2 on v1

--- a/solution.py
+++ b/solution.py
@@ -15,17 +15,19 @@
 
 
 def kernel(
-    ids_ref, gates_ref, cot_ref, hidden_ref, weight_ref, prev_ref,
-    mixed_ref, prob_ref, next_ref, psi_ref,
-    cbuf, meta, prod, rbuf, obuf, rx, mt, key_buf, part, pg, rs_out, rs_in, pg_out, pg_in, phi, phi_out, phi_in,
+    ids_ref, gates_ref, cot_ref, hidden_hbm, weight_hbm, prev_hbm,
+    mixed_ref, prob_ref, next_hbm, psi_hbm,
+    cbuf, meta, prod, rbuf, obuf, rx, mt, mtt, key_buf, part, pg, rs_out, rs_in, pg_out, pg_in, phi, phi_out, phi_in,
+    hidden_ref, weight_ref, prev_ref, next_ref, psi_ref,
     ag_send, ag_recv, meta_send, meta_recv, r_send, r_recv, o_send, o_recv,
-    rs_send, rs_recv, pg_send, pg_recv, phi_send, phi_recv,
+    rs_send, rs_recv, pg_send, pg_recv, phi_send, phi_recv, local_sem,
 ):
     tok, width = cot_ref.shape
     top = ids_ref.shape[0]
     cap = hidden_ref.shape[0] // (Q * Z)
     rows = BATCH * cap
     half = tok // 2
+    side = width // 2
     agent = lax.axis_index("agent")
     me = lax.axis_index("expert")
     z = lax.rem(me, Z)
@@ -52,6 +54,17 @@
     peers = [on_ring(1), on_ring(-1), partner] + [in_plane(p) for p in range(1, Q)]
     for peer in peers:
         pl.semaphore_signal(barrier, inc=1, device_id=peer, device_id_type=pl.DeviceIdType.MESH)
+
+    loads = [
+        pltpu.make_async_copy(src, dst, local_sem.at[i])
+        for i, (src, dst) in enumerate([
+            (hidden_hbm, hidden_ref), (weight_hbm, weight_ref), (cot_ref, cbuf.at[z]), (prev_hbm, prev_ref),
+        ])
+    ]
+    for load in loads:
+        load.start()
+    meta[z, 0:top, :] = ids_ref[...].astype(F32).astype(BF)
+    meta[z, top:2 * top, :] = gates_ref[...].astype(BF)
     pl.semaphore_wait(barrier, len(peers))
 
     def remote(src, dst, send, recv, peer):
@@ -97,10 +110,9 @@
                 if way not in meta_ways(step):
                     meta_copy(way, step - 1).wait_recv()
 
-    meta[z, 0:top, :] = ids_ref[...].astype(F32)
-    meta[z, top:2 * top, :] = gates_ref[...]
     gather_step(1)
-    cbuf[z] = cot_ref[...]
+    loads[0].wait()
+    loads[1].wait()
 
     def rows_copy(p):
         return remote(prod.at[peer_column(p)], rbuf.at[column], r_send.at[p], r_recv.at[p], in_plane(p))
@@ -134,16 +146,16 @@
     def slots(order):
         return pl.ds(pl.multiple_of(batch_at(order) * rows, rows), rows)
 
-    def out_copy(order, p):
-        return remote(obuf.at[peer_column(p), slots(order), :], rx.at[column, slots(order), :],
-                      o_send.at[order, p], o_recv.at[order, p], in_plane(p))
+    def out_copy(order, p, part_of):
+        return remote(obuf.at[part_of, peer_column(p), slots(order), :], rx.at[part_of, column, slots(order), :],
+                      o_send.at[part_of, order, p], o_recv.at[part_of, order, p], in_plane(p))
 
     def select(order):
         batch = batch_at(order)
         named, weights = [], []
         for i in range(BATCH):
-            ids = meta[batch * BATCH + i, 0:top, :]
-            gates = meta[batch * BATCH + i, top:2 * top, :]
+            about = meta[batch * BATCH + i].astype(F32)
+            ids, gates = about[0:top, :], about[top:2 * top, :]
             hit = jnp.zeros((Q, tok), F32)
             share = jnp.zeros((Q, tok), F32)
             for k in range(top):
@@ -156,37 +168,44 @@
         for i in range(BATCH):
             key = jnp.where(named[i] > 0.5, rank[i * Q:(i + 1) * Q, :] + float(i * cap), -1.0)
             key_buf[batch * BATCH + i] = key
-            for q in range(Q):
-                chosen = jnp.where(row_of == key[q:q + 1, :], weights[i][q:q + 1, :], 0.0)
-                mt[batch, pl.ds(q * rows, rows), pl.ds(i * tok, tok)] = chosen.astype(BF)
-
-    def dispatch(order):
+            chosen = jnp.concatenate(
+                [jnp.where(row_of == key[q:q + 1, :], weights[i][q:q + 1, :], 0.0) for q in range(Q)], axis=0
+            )
+            mt[batch, :, pl.ds(i * tok, tok)] = chosen.astype(BF)
+            mtt[batch, pl.ds(i * tok, tok), :] = chosen.T.astype(BF)
+
+    def build_out(order):
         batch = batch_at(order)
-        select(order)
 
         def chunk(n, carry):
             cols = pl.ds(pl.multiple_of(n * 256, 256), 256)
             tokens = cbuf[pl.ds(batch * BATCH, BATCH), :, cols].reshape(BATCH * tok, 256)
             out = jnp.dot(mt[batch], tokens, preferred_element_type=F32).astype(BF)
-            obuf[:, slots(order), cols] = out.reshape(Q, rows, 256)
+            inner = pl.ds(pl.multiple_of(lax.rem(n, side // 256) * 256, 256), 256)
+            obuf[lax.div(n, side // 256), :, slots(order), inner] = out.reshape(Q, rows, 256)
             return carry
 
         lax.fori_loop(0, width // 256, chunk, 0)
+
+    def send_out(order, part_of):
         for p in range(1, Q):
-            out_copy(order, p).start()
-        rx[column, slots(order), :] = obuf[column, slots(order), :]
-
-    def combine(order):
+            out_copy(order, p, part_of).start()
+        rx[part_of, column, slots(order), :] = obuf[part_of, column, slots(order), :]
+
+    def weigh(order):
         batch = batch_at(order)
 
         def chunk(n, carry):
             cols = pl.ds(pl.multiple_of(n * 256, 256), 256)
             arrived = rbuf[:, slots(order), cols].reshape(Q * rows, 256)
-            out = lax.dot_general(mt[batch], arrived, (((0,), (0,)), ((), ())), preferred_element_type=F32)
+            out = jnp.dot(mtt[batch], arrived, preferred_element_type=F32)
             part[pl.ds(batch * BATCH, BATCH), :, cols] = out.reshape(BATCH, tok, 256)
             return carry
 
         lax.fori_loop(0, width // 256, chunk, 0)
+
+    def score(order):
+        batch = batch_at(order)
         for i in range(BATCH):
             source = batch * BATCH + i
             scores = lax.dot_general(
@@ -194,7 +213,7 @@
                 (((1,), (1,)), ((), ())), preferred_element_type=F32,
             )
             key = key_buf[source]
-            ids = meta[source, 0:top, :]
+            ids = meta[source].astype(F32)[0:top, :]
             total = jnp.zeros((top, tok), F32)
             for q in range(Q):
                 picked = jnp.where(row_of == key[q:q + 1, :], scores[q * rows:(q + 1) * rows, :], 0.0)
@@ -202,27 +221,6 @@
                 total = total + jnp.where(ids == (z + q * Z).astype(F32), value, 0.0)
             pg[source] = total
 
-    gather_step(2)
-    gather_step(3)
-    gather_step(4)
-    dispatch(0)
-    gather_step(5)
-    gather_step(6)
-    dispatch(1)
-    gather_step(7)
-    gather_step(8)
-    dispatch(2)
-    for p in range(1, Q):
-        rows_copy(p).wait_recv()
-    for order in range(3):
-        combine(order)
-    for way in meta_ways(HALF):
-        meta_copy(way, HALF).wait_recv()
-    for way, piece in gather_pieces(HALF):
-        gather_copy(way, HALF, piece).wait_recv()
-    dispatch(3)
-    combine(3)
-
     def scatter_copy(way, step, piece):
         span = pl.ds(piece * half, half)
         return remote(rs_out.at[way, step - 1, span, :], rs_in.at[way, step - 1, span, :],
@@ -244,11 +242,13 @@
             there = block(HALF + 1 - step if way == 0 else step - HALF - 1)
             span = pl.ds(piece * half, half)
             value = part[there, span, :]
-            if (way, piece) in scatter_pieces(step - 1) and step > 1:
+            if step > 1 and (way, piece) in scatter_pieces(step - 1):
                 scatter_copy(way, step - 1, piece).wait_recv()
                 value = value + rs_in[way, step - 2, span, :].astype(F32)
             rs_out[way, step - 1, span, :] = value.astype(BF)
             scatter_copy(way, step, piece).start()
+
+    def pg_step(step):
         for way in pg_ways(step):
             there = block(HALF + 1 - step if way == 0 else step - HALF - 1)
             value = pg[there]
@@ -258,36 +258,102 @@
             pg_out[way, step - 1] = value
             pg_copy(way, step).start()
 
-    def phi_copy(i):
-        span = pl.ds(i * 128, 128)
-        return remote(phi_out.at[span, :], phi_in.at[span, :], phi_send.at[i], phi_recv.at[i], partner)
-
-    phis = hidden_ref.shape[1] // 128
+    def phi_copy(part_of):
+        return remote(phi_out.at[part_of], phi_in.at[part_of], phi_send.at[part_of], phi_recv.at[part_of], partner)
+
+    inner = hidden_ref.shape[1]
+
+    def psi_store(part_of):
+        cols = pl.ds(part_of * side, side)
+        return pltpu.make_async_copy(psi_ref.at[:, cols], psi_hbm.at[:, cols], local_sem.at[4 + part_of])
+
+    def next_store(part_of):
+        cols = pl.ds(part_of * side, side)
+        return pltpu.make_async_copy(next_ref.at[:, cols], next_hbm.at[:, cols], local_sem.at[6 + part_of])
+
+    def update(part_of):
+        for order in range(BATCHES):
+            for p in range(1, Q):
+                out_copy(order, p, part_of).wait_recv()
+        cols = pl.ds(part_of * side, side)
+        for i in range(inner // 128):
+            span = pl.ds(i * 128, 128)
+            gradient = lax.dot_general(
+                hidden_ref[:, span], rx[part_of].reshape(Q * Z * cap, side), (((0,), (0,)), ((), ())),
+                preferred_element_type=F32,
+            )
+            weight = weight_ref[span, cols].astype(F32)
+            psi = (weight - STEP_RATE * gradient).astype(BF)
+            psi_ref[span, cols] = psi
+            own = psi.astype(F32) + (weight - prev_ref[span, cols].astype(F32))
+            phi[part_of, span, :] = own
+            phi_out[part_of, span, :] = own.astype(BF)
+        phi_copy(part_of).start()
+        psi_store(part_of).start()
+
+    def mean(part_of):
+        phi_copy(part_of).wait_recv()
+        cols = pl.ds(part_of * side, side)
+        next_ref[:, cols] = (0.5 * (phi[part_of] + phi_in[part_of].astype(F32))).astype(BF)
+        next_store(part_of).start()
+
+    gather_step(2)
+    loads[2].wait()
+    loads[3].wait()
+    gather_step(3)
+    gather_step(4)
+    select(0)
+    build_out(0)
+    gather_step(5)
+    gather_step(6)
+    select(1)
+    build_out(1)
+    gather_step(7)
+    send_out(0, 0)
+    send_out(1, 0)
+    gather_step(8)
+    for way in meta_ways(HALF):
+        meta_copy(way, HALF).wait_recv()
+    select(3)
+    for p in range(1, Q):
+        rows_copy(p).wait_recv()
+    weigh(3)
     scatter_step(1)
+    select(2)
+    build_out(2)
+    send_out(2, 0)
+    for way, piece in gather_pieces(HALF):
+        gather_copy(way, HALF, piece).wait_recv()
+    build_out(3)
+    send_out(3, 0)
+    for order in range(BATCHES):
+        send_out(order, 1)
+    weigh(2)
     scatter_step(2)
+    score(3)
+    pg_step(1)
+    score(2)
     scatter_step(3)
-    for order in range(BATCHES):
-        for p in range(1, Q):
-            out_copy(order, p).wait_recv()
-    for i in range(phis):
-        span = pl.ds(i * 128, 128)
-        gradient = lax.dot_general(
-            hidden_ref[:, span], rx[...].reshape(Q * Z * cap, width), (((0,), (0,)), ((), ())),
-            preferred_element_type=F32,
-        )
-        weight = weight_ref[span, :].astype(F32)
-        psi = (weight - STEP_RATE * gradient).astype(BF)
-        psi_ref[span, :] = psi
-        own = psi.astype(F32) + (weight - prev_ref[span, :].astype(F32))
-        phi[span, :] = own
-        phi_out[span, :] = own.astype(BF)
-        phi_copy(i).start()
-    for step in range(4, HALF + 1):
-        scatter_step(step)
-    for i in range(phis):
-        span = pl.ds(i * 128, 128)
-        phi_copy(i).wait_recv()
-        next_ref[span, :] = (0.5 * (phi[span, :] + phi_in[span, :].astype(F32))).astype(BF)
+    pg_step(2)
+    weigh(1)
+    scatter_step(4)
+    pg_step(3)
+    update(0)
+    score(1)
+    weigh(0)
+    scatter_step(5)
+    pg_step(4)
+    score(0)
+    scatter_step(6)
+    pg_step(5)
+    scatter_step(7)
+    pg_step(6)
+    update(1)
+    scatter_step(8)
+    pg_step(7)
+    mean(0)
+    pg_step(8)
+    mean(1)
     for way, piece in scatter_pieces(HALF):
         scatter_copy(way, HALF, piece).wait_recv()
     for way in pg_ways(HALF):
@@ -309,9 +375,27 @@
     for p in range(1, Q):
         rows_copy(p).wait_send()
         for order in range(BATCHES):
-            out_copy(order, p).wait_send()
-    for i in range(phis):
-        phi_copy(i).wait_send()
+            for part_of in range(2):
+                out_copy(order, p, part_of).wait_send()
+    for part_of in range(2):
+        phi_copy(part_of).wait_send()
+        psi_store(part_of).wait()
+        next_store(part_of).wait()
+
+
+def hand_out(*refs):
+    count = (len(refs) - 1) // 3
+    sem = refs[-1]
+    operands, results, held = refs[:count], refs[count:2 * count], refs[2 * count:3 * count]
+    into = [pltpu.make_async_copy(operands[i], held[i], sem.at[0, i]) for i in range(count)]
+    out = [pltpu.make_async_copy(held[i], results[i], sem.at[1, i]) for i in range(count)]
+    for copy in into:
+        copy.start()
+    for i in range(count):
+        into[i].wait()
+        out[i].start()
+    for copy in out:
+        copy.wait()
 
 
 def per_device(expert_ids, gate_probs, cotangent, hidden, w_down, psi_prev):
@@ -320,26 +404,28 @@
     slot_count, inner = hidden.shape[2:]
     cap = slot_count // (Q * Z)
     rows = BATCH * cap
-    vmem = pl.BlockSpec(memory_space=pltpu.VMEM)
+    vmem, anywhere = pl.BlockSpec(memory_space=pltpu.VMEM), pl.BlockSpec(memory_space=pl.ANY)
     dma = pltpu.SemaphoreType.DMA
-    mixed, prob, w_next, psi_next = pl.pallas_call(
+    shapes = (
+        jax.ShapeDtypeStruct((tok, width), BF),
+        jax.ShapeDtypeStruct((top, tok), F32),
+        jax.ShapeDtypeStruct((inner, width), BF),
+        jax.ShapeDtypeStruct((inner, width), BF),
+    )
+    made = pl.pallas_call(
         kernel,
-        out_shape=(
-            jax.ShapeDtypeStruct((tok, width), BF),
-            jax.ShapeDtypeStruct((top, tok), F32),
-            jax.ShapeDtypeStruct((inner, width), BF),
-            jax.ShapeDtypeStruct((inner, width), BF),
-        ),
-        in_specs=[vmem] * 6,
-        out_specs=(vmem,) * 4,
+        out_shape=shapes,
+        in_specs=[vmem] * 2 + [anywhere] * 4,
+        out_specs=(vmem, vmem, anywhere, anywhere),
         scratch_shapes=[
             pltpu.VMEM((Z, tok, width), BF),
-            pltpu.VMEM((Z, 2 * top, tok), F32),
+            pltpu.VMEM((Z, 2 * top, tok), BF),
             pltpu.VMEM((Q, Z * cap, width), BF),
             pltpu.VMEM((Q, Z * cap, width), BF),
-            pltpu.VMEM((Q, Z * cap, width), BF),
-            pltpu.VMEM((Q, Z * cap, width), BF),
+            pltpu.VMEM((2, Q, Z * cap, width // 2), BF),
+            pltpu.VMEM((2, Q, Z * cap, width // 2), BF),
             pltpu.VMEM((BATCHES, Q * rows, BATCH * tok), BF),
+            pltpu.VMEM((BATCHES, BATCH * tok, Q * rows), BF),
             pltpu.VMEM((Z, Q, tok), F32),
             pltpu.VMEM((Z, tok, width), F32),
             pltpu.VMEM((Z, top, tok), F32),
@@ -347,21 +433,34 @@
             pltpu.VMEM((2, HALF, tok, width), BF),
             pltpu.VMEM((2, HALF, top, tok), F32),
             pltpu.VMEM((2, HALF, top, tok), F32),
-            pltpu.VMEM((inner, width), F32),
+            pltpu.VMEM((2, inner, width // 2), F32),
+            pltpu.VMEM((2, inner, width // 2), BF),
+            pltpu.VMEM((2, inner, width // 2), BF),
+            pltpu.VMEM((slot_count, inner), BF),
+            pltpu.VMEM((inner, width), BF),
+            pltpu.VMEM((inner, width), BF),
             pltpu.VMEM((inner, width), BF),
             pltpu.VMEM((inner, width), BF),
             dma((2, HALF, 2)), dma((2, HALF, 2)),
             dma((2, HALF)), dma((2, HALF)),
             dma((Q,)), dma((Q,)),
-            dma((BATCHES, Q)), dma((BATCHES, Q)),
+            dma((2, BATCHES, Q)), dma((2, BATCHES, Q)),
             dma((2, HALF, 2)), dma((2, HALF, 2)),
             dma((2, HALF)), dma((2, HALF)),
-            dma((inner // 128,)), dma((inner // 128,)),
+            dma((2,)), dma((2,)),
+            dma((8,)),
         ],
         compiler_params=pltpu.CompilerParams(
             collective_id=0, has_side_effects=True, vmem_limit_bytes=60 * 1024 * 1024,
         ),
     )(expert_ids[0].T, gate_probs[0].T, cotangent[0], hidden[0, 0], w_down[0, 0], psi_prev[0, 0])
+    mixed, prob, w_next, psi_next = pl.pallas_call(
+        hand_out,
+        out_shape=shapes,
+        in_specs=[anywhere] * 4,
+        out_specs=(anywhere,) * 4,
+        scratch_shapes=[pltpu.VMEM(shape.shape, shape.dtype) for shape in shapes] + [dma((2, 4))],
+    )(*made)
     return mixed[None], prob.T[None], w_next[None, None], psi_next[None, None]
 
 

time: 129 us -> 115 us (0.89)
  the two profiles are of different devices: /device:TPU:8 before, /device:TPU:4 now
where the time goes in v2:
time: 115 us
  Pallas kernels  114 us (99%)
    pallas_call x1, Pallas kernels, per_device(): pl.pallas_call(kernel, out_shape=shapes, in_specs=[vmem] * 2 + [anywhere]...  112 us
    pallas_call x1, Pallas kernels, per_device(): pl.pallas_call(hand_out, out_shape=shapes, in_specs=[anywhere] * 4, out_s...  2.43 us

profile of v2, /device:TPU:4, one launch (start us, length us, event | category | flops | bytes accessed | tf_op | source)
XLA Modules:
  0.0 114.6 jit_solution(17551855236148053240)
XLA Ops:
  0.6 111.5 %shard_map.93 = (bf16[128,1024]{1,0:T(8,128)(2,1)}, f32[8,128]{1,0:T(8,128)}, bf16[384,1024]{1,0:T(8,128)(2,1)}, bf16[384,1024]{1,0:T(8,128)(2,1)}) custom-call(s32[8,128]{1,0:T(8,128)} %bitcast.20, f32[8,128]{1,0:T(8,128)} %bitcast.21, bf16[128,1024]{1,0:T(8,128)(2,1)} %bitcast.19, bf16[1536,384]{1,0:T(8,128)(2,1)} %bitcast.16, bf16[384,1024]{1,0:T(8,128)(2,1)} %bitcast.17, ...), custom_call_target="tpu_custom_call" | custom-call | tf_op jit(solution)/shard_map/pallas_call | solution.py:415
  112.2 2.4 %shard_map.94 = (bf16[128,1024]{1,0:T(8,128)(2,1)}, f32[8,128]{1,0:T(8,128)}, bf16[384,1024]{1,0:T(8,128)(2,1)}, bf16[384,1024]{1,0:T(8,128)(2,1)}) custom-call(bf16[128,1024]{1,0:T(8,128)(2,1)} %get-tuple-element.12.refs_0_, f32[8,128]{1,0:T(8,128)} %get-tuple-element.13.refs_1_, bf16[384,1024]{1,0:T(8,128)(2,1)} %get-tuple-element.14.refs_2_, ...), custom_call_target="tpu_custom_call" | custom-call | tf_op jit(solution)/shard_map/pallas_call | solution.py:457

commit v3 on v2

--- a/solution.py
+++ b/solution.py
@@ -15,15 +15,15 @@
 
 
 def kernel(
-    ids_ref, gates_ref, cot_ref, hidden_hbm, weight_hbm, prev_hbm,
+    ids_hbm, gates_hbm, cot_ref, hidden_hbm, weight_hbm, prev_hbm,
     mixed_ref, prob_ref, next_hbm, psi_hbm,
     cbuf, meta, prod, rbuf, obuf, rx, mt, mtt, key_buf, part, pg, rs_out, rs_in, pg_out, pg_in, phi, phi_out, phi_in,
-    hidden_ref, weight_ref, prev_ref, next_ref, psi_ref,
+    ids_ref, gates_ref, hidden_ref, weight_ref, prev_ref, next_ref, psi_ref,
     ag_send, ag_recv, meta_send, meta_recv, r_send, r_recv, o_send, o_recv,
     rs_send, rs_recv, pg_send, pg_recv, phi_send, phi_recv, local_sem,
 ):
     tok, width = cot_ref.shape
-    top = ids_ref.shape[0]
+    top = ids_hbm.shape[0]
     cap = hidden_ref.shape[0] // (Q * Z)
     rows = BATCH * cap
     half = tok // 2
@@ -58,13 +58,12 @@
     loads = [
         pltpu.make_async_copy(src, dst, local_sem.at[i])
         for i, (src, dst) in enumerate([
-            (hidden_hbm, hidden_ref), (weight_hbm, weight_ref), (cot_ref, cbuf.at[z]), (prev_hbm, prev_ref),
+            (ids_hbm, ids_ref), (gates_hbm, gates_ref), (hidden_hbm, hidden_ref), (weight_hbm, weight_ref),
+            (cot_ref, cbuf.at[z]), (prev_hbm, prev_ref),
         ])
     ]
     for load in loads:
         load.start()
-    meta[z, 0:top, :] = ids_ref[...].astype(F32).astype(BF)
-    meta[z, top:2 * top, :] = gates_ref[...].astype(BF)
     pl.semaphore_wait(barrier, len(peers))
 
     def remote(src, dst, send, recv, peer):
@@ -93,26 +92,29 @@
     def meta_ways(step):
         return [0] if step == HALF else [0, 1]
 
-    def gather_step(step):
-        for way in meta_ways(step):
-            if step > 1:
-                meta_copy(way, step - 1).wait_recv()
+    def meta_hop(way, step):
+        if step > 1 and way in meta_ways(step - 1):
+            meta_copy(way, step - 1).wait_recv()
+        if way in meta_ways(step):
             meta_copy(way, step).start()
-        for way, piece in gather_pieces(step):
+
+    def gather_pair(step, pair, about=0):
+        for way in (0, 1):
+            piece = way if pair == 0 else 1 - way
             if step > 1:
                 gather_copy(way, step - 1, piece).wait_recv()
+            if about:
+                meta_hop(way, about)
             gather_copy(way, step, piece).start()
-        if step > 1:
-            for way, piece in gather_pieces(step - 1):
-                if (way, piece) not in gather_pieces(step):
-                    gather_copy(way, step - 1, piece).wait_recv()
-            for way in meta_ways(step - 1):
-                if way not in meta_ways(step):
-                    meta_copy(way, step - 1).wait_recv()
-
-    gather_step(1)
+
+    gather_pair(1, 0)
     loads[0].wait()
     loads[1].wait()
+    meta[z, 0:top, :] = ids_ref[...].astype(F32).astype(BF)
+    meta[z, top:2 * top, :] = gates_ref[...].astype(BF)
+    gather_pair(1, 1, about=1)
+    loads[2].wait()
+    loads[3].wait()
 
     def rows_copy(p):
         return remote(prod.at[peer_column(p)], rbuf.at[column], r_send.at[p], r_recv.at[p], in_plane(p))
@@ -237,8 +239,19 @@
     def pg_ways(step):
         return [0] if step == 1 else [0, 1]
 
-    def scatter_step(step):
-        for way, piece in scatter_pieces(step):
+    def pg_hop(way, step):
+        if way not in pg_ways(step):
+            return
+        value = pg[block(HALF + 1 - step if way == 0 else step - HALF - 1)]
+        if step > 1 and way in pg_ways(step - 1):
+            pg_copy(way, step - 1).wait_recv()
+            value = value + pg_in[way, step - 2]
+        pg_out[way, step - 1] = value
+        pg_copy(way, step).start()
+
+    def scatter_pair(step, pair, score_step=0):
+        for way in (0, 1):
+            piece = way if pair == 0 else 1 - way
             there = block(HALF + 1 - step if way == 0 else step - HALF - 1)
             span = pl.ds(piece * half, half)
             value = part[there, span, :]
@@ -246,17 +259,9 @@
                 scatter_copy(way, step - 1, piece).wait_recv()
                 value = value + rs_in[way, step - 2, span, :].astype(F32)
             rs_out[way, step - 1, span, :] = value.astype(BF)
+            if score_step:
+                pg_hop(way, score_step)
             scatter_copy(way, step, piece).start()
-
-    def pg_step(step):
-        for way in pg_ways(step):
-            there = block(HALF + 1 - step if way == 0 else step - HALF - 1)
-            value = pg[there]
-            if step > 1 and way in pg_ways(step - 1):
-                pg_copy(way, step - 1).wait_recv()
-                value = value + pg_in[way, step - 2]
-            pg_out[way, step - 1] = value
-            pg_copy(way, step).start()
 
     def phi_copy(part_of):
         return remote(phi_out.at[part_of], phi_in.at[part_of], phi_send.at[part_of], phi_recv.at[part_of], partner)
@@ -265,11 +270,11 @@
 
     def psi_store(part_of):
         cols = pl.ds(part_of * side, side)
-        return pltpu.make_async_copy(psi_ref.at[:, cols], psi_hbm.at[:, cols], local_sem.at[4 + part_of])
+        return pltpu.make_async_copy(psi_ref.at[:, cols], psi_hbm.at[:, cols], local_sem.at[6 + part_of])
 
     def next_store(part_of):
         cols = pl.ds(part_of * side, side)
-        return pltpu.make_async_copy(next_ref.at[:, cols], next_hbm.at[:, cols], local_sem.at[6 + part_of])
+        return pltpu.make_async_copy(next_ref.at[:, cols], next_hbm.at[:, cols], local_sem.at[8 + part_of])
 
     def update(part_of):
         for order in range(BATCHES):
@@ -297,71 +302,80 @@
         next_ref[:, cols] = (0.5 * (phi[part_of] + phi_in[part_of].astype(F32))).astype(BF)
         next_store(part_of).start()
 
-    gather_step(2)
-    loads[2].wait()
-    loads[3].wait()
-    gather_step(3)
-    gather_step(4)
+    gather_pair(2, 0, about=2)
+    gather_pair(2, 1, about=3)
+    loads[4].wait()
+    loads[5].wait()
+    gather_pair(3, 0, about=4)
+    gather_pair(3, 1, about=5)
+    gather_pair(4, 0, about=6)
+    gather_pair(4, 1, about=7)
     select(0)
     build_out(0)
-    gather_step(5)
-    gather_step(6)
+    send_out(0, 0)
+    gather_pair(5, 0, about=8)
+    gather_pair(5, 1)
+    meta_copy(0, HALF).wait_recv()
     select(1)
+    gather_pair(6, 0)
+    gather_pair(6, 1)
     build_out(1)
-    gather_step(7)
-    send_out(0, 0)
     send_out(1, 0)
-    gather_step(8)
-    for way in meta_ways(HALF):
-        meta_copy(way, HALF).wait_recv()
+    gather_pair(7, 0)
+    gather_pair(7, 1)
+    select(2)
     select(3)
+    gather_pair(8, 0)
+    for way in (0, 1):
+        gather_copy(way, HALF - 1, 1 - way).wait_recv()
+    build_out(2)
     for p in range(1, Q):
         rows_copy(p).wait_recv()
     weigh(3)
-    scatter_step(1)
-    select(2)
-    build_out(2)
+    scatter_pair(1, 0)
     send_out(2, 0)
+    weigh(2)
+    scatter_pair(2, 1)
     for way, piece in gather_pieces(HALF):
         gather_copy(way, HALF, piece).wait_recv()
     build_out(3)
     send_out(3, 0)
-    for order in range(BATCHES):
-        send_out(order, 1)
-    weigh(2)
-    scatter_step(2)
+    scatter_pair(2, 0)
+    send_out(0, 1)
+    send_out(1, 1)
+    scatter_pair(3, 1)
+    send_out(2, 1)
+    send_out(3, 1)
+    scatter_pair(3, 0)
+    weigh(1)
     score(3)
-    pg_step(1)
+    scatter_pair(4, 1, score_step=1)
     score(2)
-    scatter_step(3)
-    pg_step(2)
-    weigh(1)
-    scatter_step(4)
-    pg_step(3)
+    scatter_pair(4, 0, score_step=2)
     update(0)
+    scatter_pair(5, 1, score_step=3)
     score(1)
+    scatter_pair(5, 0, score_step=4)
     weigh(0)
-    scatter_step(5)
-    pg_step(4)
+    scatter_pair(6, 1, score_step=5)
     score(0)
-    scatter_step(6)
-    pg_step(5)
-    scatter_step(7)
-    pg_step(6)
+    scatter_pair(6, 0, score_step=6)
+    scatter_pair(7, 1, score_step=7)
+    scatter_pair(7, 0, score_step=8)
     update(1)
-    scatter_step(8)
-    pg_step(7)
+    scatter_pair(8, 1)
     mean(0)
-    pg_step(8)
+    scatter_pair(8, 0)
     mean(1)
-    for way, piece in scatter_pieces(HALF):
-        scatter_copy(way, HALF, piece).wait_recv()
     for way in pg_ways(HALF):
         pg_copy(way, HALF).wait_recv()
+    prob_ref[...] = pg[z] + pg_in[0, HALF - 1] + pg_in[1, HALF - 1]
+    for pair in (1, 0):
+        for way in (0, 1):
+            scatter_copy(way, HALF, way if pair == 0 else 1 - way).wait_recv()
     mixed_ref[...] = (
         part[z] + rs_in[0, HALF - 1].astype(F32) + rs_in[1, HALF - 1].astype(F32)
     ).astype(BF)
-    prob_ref[...] = pg[z] + pg_in[0, HALF - 1] + pg_in[1, HALF - 1]
 
     for step in range(1, HALF + 1):
         for way, piece in gather_pieces(step):
@@ -415,7 +429,7 @@
     made = pl.pallas_call(
         kernel,
         out_shape=shapes,
-        in_specs=[vmem] * 2 + [anywhere] * 4,
+        in_specs=[anywhere] * 6,
         out_specs=(vmem, vmem, anywhere, anywhere),
         scratch_shapes=[
             pltpu.VMEM((Z, tok, width), BF),
@@ -436,6 +450,8 @@
             pltpu.VMEM((2, inner, width // 2), F32),
             pltpu.VMEM((2, inner, width // 2), BF),
             pltpu.VMEM((2, inner, width // 2), BF),
+            pltpu.VMEM((top, tok), jnp.int32),
+            pltpu.VMEM((top, tok), F32),
             pltpu.VMEM((slot_count, inner), BF),
             pltpu.VMEM((inner, width), BF),
             pltpu.VMEM((inner, width), BF),
@@ -448,7 +464,7 @@
             dma((2, HALF, 2)), dma((2, HALF, 2)),
             dma((2, HALF)), dma((2, HALF)),
             dma((2,)), dma((2,)),
-            dma((8,)),
+            dma((10,)),
         ],
         compiler_params=pltpu.CompilerParams(
             collective_id=0, has_side_effects=True, vmem_limit_bytes=60 * 1024 * 1024,

time: 115 us -> 111 us (0.965)
  the two profiles are of different devices: /device:TPU:4 before, /device:TPU:8 now
where the time goes in v3:
time: 111 us; the launch traced here: 110 us
  Pallas kernels  110 us (99%)
    pallas_call x1, Pallas kernels, per_device(): pl.pallas_call(kernel, out_shape=shapes, in_specs=[anywhere] * 6, out_spe...  107 us
    pallas_call x1, Pallas kernels, per_device(): pl.pallas_call(hand_out, out_shape=shapes, in_specs=[anywhere] * 4, out_s...  2.43 us

profile of v3, /device:TPU:8, one launch (start us, length us, event | category | flops | bytes accessed | tf_op | source)
XLA Modules:
  0.0 110.4 jit_solution(17869381697462951668)
XLA Ops:
  0.6 107.4 %shard_map.93 = (bf16[128,1024]{1,0:T(8,128)(2,1)}, f32[8,128]{1,0:T(8,128)}, bf16[384,1024]{1,0:T(8,128)(2,1)}, bf16[384,1024]{1,0:T(8,128)(2,1)}) custom-call(s32[8,128]{1,0:T(8,128)} %bitcast.20, f32[8,128]{1,0:T(8,128)} %bitcast.21, bf16[128,1024]{1,0:T(8,128)(2,1)} %bitcast.19, bf16[1536,384]{1,0:T(8,128)(2,1)} %bitcast.16, bf16[384,1024]{1,0:T(8,128)(2,1)} %bitcast.17, ...), custom_call_target="tpu_custom_call" | custom-call | tf_op jit(solution)/shard_map/pallas_call | solution.py:429
  108.0 2.4 %shard_map.94 = (bf16[128,1024]{1,0:T(8,128)(2,1)}, f32[8,128]{1,0:T(8,128)}, bf16[384,1024]{1,0:T(8,128)(2,1)}, bf16[384,1024]{1,0:T(8,128)(2,1)}) custom-call(bf16[128,1024]{1,0:T(8,128)(2,1)} %get-tuple-element.12.refs_0_, f32[8,128]{1,0:T(8,128)} %get-tuple-element.13.refs_1_, bf16[384,1024]{1,0:T(8,128)(2,1)} %get-tuple-element.14.refs_2_, ...), custom_call_target="tpu_custom_call" | custom-call | tf_op jit(solution)/shard_map/pallas_call | solution.py:473

commit v4 on v3

--- a/solution.py
+++ b/solution.py
@@ -16,9 +16,9 @@
 
 def kernel(
     ids_hbm, gates_hbm, cot_ref, hidden_hbm, weight_hbm, prev_hbm,
-    mixed_ref, prob_ref, next_hbm, psi_hbm,
+    mixed_ref, prob_ref, next_ref, psi_ref,
     cbuf, meta, prod, rbuf, obuf, rx, mt, mtt, key_buf, part, pg, rs_out, rs_in, pg_out, pg_in, phi, phi_out, phi_in,
-    ids_ref, gates_ref, hidden_ref, weight_ref, prev_ref, next_ref, psi_ref,
+    ids_ref, gates_ref, hidden_ref, weight_ref, prev_ref,
     ag_send, ag_recv, meta_send, meta_recv, r_send, r_recv, o_send, o_recv,
     rs_send, rs_recv, pg_send, pg_recv, phi_send, phi_recv, local_sem,
 ):
@@ -268,14 +268,6 @@
 
     inner = hidden_ref.shape[1]
 
-    def psi_store(part_of):
-        cols = pl.ds(part_of * side, side)
-        return pltpu.make_async_copy(psi_ref.at[:, cols], psi_hbm.at[:, cols], local_sem.at[6 + part_of])
-
-    def next_store(part_of):
-        cols = pl.ds(part_of * side, side)
-        return pltpu.make_async_copy(next_ref.at[:, cols], next_hbm.at[:, cols], local_sem.at[8 + part_of])
-
     def update(part_of):
         for order in range(BATCHES):
             for p in range(1, Q):
@@ -294,13 +286,11 @@
             phi[part_of, span, :] = own
             phi_out[part_of, span, :] = own.astype(BF)
         phi_copy(part_of).start()
-        psi_store(part_of).start()
 
     def mean(part_of):
         phi_copy(part_of).wait_recv()
         cols = pl.ds(part_of * side, side)
         next_ref[:, cols] = (0.5 * (phi[part_of] + phi_in[part_of].astype(F32))).astype(BF)
-        next_store(part_of).start()
 
     gather_pair(2, 0, about=2)
     gather_pair(2, 1, about=3)
@@ -393,22 +383,15 @@
                 out_copy(order, p, part_of).wait_send()
     for part_of in range(2):
         phi_copy(part_of).wait_send()
-        psi_store(part_of).wait()
-        next_store(part_of).wait()
 
 
 def hand_out(*refs):
-    count = (len(refs) - 1) // 3
+    count = (len(refs) - 1) // 2
     sem = refs[-1]
-    operands, results, held = refs[:count], refs[count:2 * count], refs[2 * count:3 * count]
-    into = [pltpu.make_async_copy(operands[i], held[i], sem.at[0, i]) for i in range(count)]
-    out = [pltpu.make_async_copy(held[i], results[i], sem.at[1, i]) for i in range(count)]
-    for copy in into:
+    copies = [pltpu.make_async_copy(refs[i], refs[count + i], sem.at[i]) for i in range(count)]
+    for copy in copies:
         copy.start()
-    for i in range(count):
-        into[i].wait()
-        out[i].start()
-    for copy in out:
+    for copy in copies:
         copy.wait()
 
 
@@ -428,9 +411,9 @@
     )
     made = pl.pallas_call(
         kernel,
-        out_shape=shapes,
+        out_shape=tuple(pltpu.VMEM(shape.shape, shape.dtype) for shape in shapes),
         in_specs=[anywhere] * 6,
-        out_specs=(vmem, vmem, anywhere, anywhere),
+        out_specs=(vmem,) * 4,
         scratch_shapes=[
             pltpu.VMEM((Z, tok, width), BF),
             pltpu.VMEM((Z, 2 * top, tok), BF),
@@ -455,8 +438,6 @@
             pltpu.VMEM((slot_count, inner), BF),
             pltpu.VMEM((inner, width), BF),
             pltpu.VMEM((inner, width), BF),
-            pltpu.VMEM((inner, width), BF),
-            pltpu.VMEM((inner, width), BF),
             dma((2, HALF, 2)), dma((2, HALF, 2)),
             dma((2, HALF)), dma((2, HALF)),
             dma((Q,)), dma((Q,)),
@@ -464,7 +445,7 @@
             dma((2, HALF, 2)), dma((2, HALF, 2)),
             dma((2, HALF)), dma((2, HALF)),
             dma((2,)), dma((2,)),
-            dma((10,)),
+            dma((6,)),
         ],
         compiler_params=pltpu.CompilerParams(
             collective_id=0, has_side_effects=True, vmem_limit_bytes=60 * 1024 * 1024,
@@ -475,8 +456,8 @@
         out_shape=shapes,
         in_specs=[anywhere] * 4,
         out_specs=(anywhere,) * 4,
-        scratch_shapes=[pltpu.VMEM(shape.shape, shape.dtype) for shape in shapes] + [dma((2, 4))],
-    )(*made)
+        scratch_shapes=[dma((4,))],
+    )(*(pltpu.with_memory_space_constraint(part, pltpu.VMEM) for part in made))
     return mixed[None], prob.T[None], w_next[None, None], psi_next[None, None]
 
 

time: 111 us -> 108 us (0.973)
  Pallas kernels: 110 us -> 107 us
    pallas_call x1, Pallas kernels: 107 us -> 106 us  [per_device(): pl.pallas_call(kernel, out_shape=tuple((pltpu.VMEM(shape.shape, shape.dty...]
    pallas_call x1, Pallas kernels: 2.43 us -> 1.27 us  [per_device(): pl.pallas_call(hand_out, out_shape=shapes, in_specs=[anywhere] * 4, out_s...]
where the time goes in v4:
time: 108 us
  Pallas kernels  107 us (99%)
    pallas_call x1, Pallas kernels, per_device(): pl.pallas_call(kernel, out_shape=tuple((pltpu.VMEM(shape.shape, shape.dty...  106 us

profile of v4, /device:TPU:8, one launch (start us, length us, event | category | flops | bytes accessed | tf_op | source)
XLA Modules:
  0.0 108.1 jit_solution(15584571768320219157)
XLA Ops:
  0.6 106.2 %shard_map.93 = (bf16[128,1024]{1,0:T(8,128)(2,1)S(1)}, f32[8,128]{1,0:T(8,128)S(1)}, bf16[384,1024]{1,0:T(8,128)(2,1)S(1)}, bf16[384,1024]{1,0:T(8,128)(2,1)S(1)}) custom-call(s32[8,128]{1,0:T(8,128)} %bitcast.20, f32[8,128]{1,0:T(8,128)} %bitcast.21, bf16[128,1024]{1,0:T(8,128)(2,1)} %bitcast.19, bf16[1536,384]{1,0:T(8,128)(2,1)} %bitcast.16, ...), custom_call_target="tpu_custom_call" | custom-call | tf_op jit(solution)/shard_map/pallas_call | solution.py:412
  106.8 1.3 %shard_map.94 = (bf16[128,1024]{1,0:T(8,128)(2,1)}, f32[8,128]{1,0:T(8,128)}, bf16[384,1024]{1,0:T(8,128)(2,1)}, bf16[384,1024]{1,0:T(8,128)(2,1)}) custom-call(bf16[128,1024]{1,0:T(8,128)(2,1)S(1)} %get-tuple-element.12.refs_0_, f32[8,128]{1,0:T(8,128)S(1)} %get-tuple-element.13.refs_1_, bf16[384,1024]{1,0:T(8,128)(2,1)S(1)} %get-tuple-element.14.refs_2_, ...), custom_call_target="tpu_custom_call" | custom-call | tf_op jit(solution)/shard_map/pallas_call | solution.py:454

commit v5 on v4

--- a/solution.py
+++ b/solution.py
@@ -116,8 +116,23 @@
     loads[2].wait()
     loads[3].wait()
 
-    def rows_copy(p):
-        return remote(prod.at[peer_column(p)], rbuf.at[column], r_send.at[p], r_recv.at[p], in_plane(p))
+    near = 1 - 2 * lax.div(3 - lax.rem(z, BATCH), 2)
+    first = lax.div(z, BATCH)
+
+    def batch_at(order):
+        shift = [0, near, -near, 2][order]
+        return lax.rem(first + shift + BATCHES, BATCHES)
+
+    def slots(order):
+        return pl.ds(pl.multiple_of(batch_at(order) * rows, rows), rows)
+
+    def rows_copy(order, p):
+        return remote(prod.at[peer_column(p), slots(order), :], rbuf.at[column, slots(order), :],
+                      r_send.at[order, p], r_recv.at[order, p], in_plane(p))
+
+    def rows_arrive(order):
+        for p in range(1, Q):
+            rows_copy(order, p).wait_recv()
 
     def produce(p):
         there = peer_column(p)
@@ -127,26 +142,20 @@
             rbuf[column] = out
         else:
             prod[there] = out
-            rows_copy(p).start()
+            rows_copy(3, p).start()
+            rows_copy(2, p).start()
 
     for p in list(range(1, Q)) + [0]:
         produce(p)
+    for order in (1, 0):
+        for p in range(1, Q):
+            rows_copy(order, p).start()
 
     lane = lax.broadcasted_iota(jnp.int32, (tok, tok), 1)
     sub = lax.broadcasted_iota(jnp.int32, (tok, tok), 0)
     earlier = (sub < lane).astype(F32).astype(BF)
     expert_of = (lax.broadcasted_iota(jnp.int32, (Q, tok), 0) * Z + z).astype(F32)
     row_of = lax.broadcasted_iota(jnp.int32, (rows, tok), 0).astype(F32)
-
-    near = 1 - 2 * lax.div(3 - lax.rem(z, BATCH), 2)
-    first = lax.div(z, BATCH)
-
-    def batch_at(order):
-        shift = [0, near, -near, 2][order]
-        return lax.rem(first + shift + BATCHES, BATCHES)
-
-    def slots(order):
-        return pl.ds(pl.multiple_of(batch_at(order) * rows, rows), rows)
 
     def out_copy(order, p, part_of):
         return remote(obuf.at[part_of, peer_column(p), slots(order), :], rx.at[part_of, column, slots(order), :],
@@ -308,24 +317,24 @@
     meta_copy(0, HALF).wait_recv()
     select(1)
     gather_pair(6, 0)
+    select(3)
     gather_pair(6, 1)
     build_out(1)
     send_out(1, 0)
     gather_pair(7, 0)
+    select(2)
+    rows_arrive(3)
+    weigh(3)
     gather_pair(7, 1)
-    select(2)
-    select(3)
+    rows_arrive(2)
+    weigh(2)
     gather_pair(8, 0)
+    scatter_pair(1, 0)
+    scatter_pair(2, 1)
     for way in (0, 1):
         gather_copy(way, HALF - 1, 1 - way).wait_recv()
     build_out(2)
-    for p in range(1, Q):
-        rows_copy(p).wait_recv()
-    weigh(3)
-    scatter_pair(1, 0)
     send_out(2, 0)
-    weigh(2)
-    scatter_pair(2, 1)
     for way, piece in gather_pieces(HALF):
         gather_copy(way, HALF, piece).wait_recv()
     build_out(3)
@@ -337,6 +346,7 @@
     send_out(2, 1)
     send_out(3, 1)
     scatter_pair(3, 0)
+    rows_arrive(1)
     weigh(1)
     score(3)
     scatter_pair(4, 1, score_step=1)
@@ -346,6 +356,7 @@
     scatter_pair(5, 1, score_step=3)
     score(1)
     scatter_pair(5, 0, score_step=4)
+    rows_arrive(0)
     weigh(0)
     scatter_pair(6, 1, score_step=5)
     score(0)
@@ -377,8 +388,8 @@
         for way in pg_ways(step):
             pg_copy(way, step).wait_send()
     for p in range(1, Q):
-        rows_copy(p).wait_send()
         for order in range(BATCHES):
+            rows_copy(order, p).wait_send()
             for part_of in range(2):
                 out_copy(order, p, part_of).wait_send()
     for part_of in range(2):
@@ -440,7 +451,7 @@
             pltpu.VMEM((inner, width), BF),
             dma((2, HALF, 2)), dma((2, HALF, 2)),
             dma((2, HALF)), dma((2, HALF)),
-            dma((Q,)), dma((Q,)),
+            dma((BATCHES, Q)), dma((BATCHES, Q)),
             dma((2, BATCHES, Q)), dma((2, BATCHES, Q)),
             dma((2, HALF, 2)), dma((2, HALF, 2)),
             dma((2, HALF)), dma((2, HALF)),

time: 108 us -> 107 us (level)
    pallas_call x1, Pallas kernels: 106 us -> 104 us  [per_device(): pl.pallas_call(kernel, out_shape=tuple((pltpu.VMEM(shape.shape, shape.dty...]
where the time goes in v5:
time: 107 us; the launch traced here: 106 us
  Pallas kernels  106 us (99%)
    pallas_call x1, Pallas kernels, per_device(): pl.pallas_call(kernel, out_shape=tuple((pltpu.VMEM(shape.shape, shape.dty...  104 us

profile of v5, /device:TPU:8, one launch (start us, length us, event | category | flops | bytes accessed | tf_op | source)
XLA Modules:
  0.0 106.4 jit_solution(7646843259305836638)
XLA Ops:
  0.6 104.3 %shard_map.93 = (bf16[128,1024]{1,0:T(8,128)(2,1)S(1)}, f32[8,128]{1,0:T(8,128)S(1)}, bf16[384,1024]{1,0:T(8,128)(2,1)S(1)}, bf16[384,1024]{1,0:T(8,128)(2,1)S(1)}) custom-call(s32[8,128]{1,0:T(8,128)} %bitcast.20, f32[8,128]{1,0:T(8,128)} %bitcast.21, bf16[128,1024]{1,0:T(8,128)(2,1)} %bitcast.19, bf16[1536,384]{1,0:T(8,128)(2,1)} %bitcast.16, ...), custom_call_target="tpu_custom_call" | custom-call | tf_op jit(solution)/shard_map/pallas_call | solution.py:423
  104.9 1.3 %shard_map.94 = (bf16[128,1024]{1,0:T(8,128)(2,1)}, f32[8,128]{1,0:T(8,128)}, bf16[384,1024]{1,0:T(8,128)(2,1)}, bf16[384,1024]{1,0:T(8,128)(2,1)}) custom-call(bf16[128,1024]{1,0:T(8,128)(2,1)S(1)} %get-tuple-element.12.refs_0_, f32[8,128]{1,0:T(8,128)S(1)} %get-tuple-element.13.refs_1_, bf16[384,1024]{1,0:T(8,128)(2,1)S(1)} %get-tuple-element.14.refs_2_, ...), custom_call_target="tpu_custom_call" | custom-call | tf_op jit(solution)/shard_map/pallas_call | solution.py:465
